TPU v7x, 512 devices: a whole 4x8x8 slice. The times are simulated.
512 devices in a mesh: row: 16 (over z, core), col: 32 (over y, x).
Axes of the slice: x: 4, y: 8, z: 8, core: 2. Of those that a mesh axis runs over, the one named last changes fastest.
Arguments:
- inverse_block: float32 [8192, 8192], P('row', 'col'), as said below
- panels: bfloat16 [2, 8192, 512], P(None, 'row'), may hold values from -0.09375 to 0.09375
- pattern: int32 [2, 64], replicated, may hold values 0 or 1
Outputs:
- inverse_panel: float32 [2, 8192, 512], P(None, ('row', 'col'))
- update: float32 [2, 512, 512], P(None, 'col')
Inputs may be any that keep to these rules, and one draw needn't show every extreme that they name: `pattern`: 1 marks a block of rows in the supernode's structure, 0 a block outside it. `inverse_block`: symmetric.
All inputs are finite; a program needn't handle non-finite values.
Results may differ from a plain program's by a relative error of at most 0.00045.
Values may be sent and summed in bfloat16 or wider, within the bound.
A program may use at most 64 MiB of HBM per device.

v0:
```python
import jax
import jax.numpy as jnp
from jax import lax
from jax.sharding import PartitionSpec as P

BLOCK = 128


def spread(block, axis, source):
    block = jnp.where(lax.axis_index(axis) == source, block, jnp.zeros_like(block))
    return lax.psum(block, axis)


def shards(inverse_block, panels, pattern):
    row_count = lax.axis_size("row")
    col_count = lax.axis_size("col")
    row_index = lax.axis_index("row")
    col_index = lax.axis_index("col")
    rows_here = panels.shape[1]
    cols_here = inverse_block.shape[1]
    ratio = col_count // row_count
    span = rows_here // col_count
    blocks = pattern.shape[1]
    row_ids = row_index * rows_here + jnp.arange(rows_here, dtype=jnp.int32)
    onehot = (row_ids // BLOCK)[:, None] == jnp.arange(blocks, dtype=jnp.int32)[None, :]
    row_mask = jnp.sum(jnp.where(onehot[None, :, :], pattern[:, None, :], 0), axis=2)
    used = panels * row_mask[:, :, None].astype(jnp.bfloat16)
    piece = lax.dynamic_slice_in_dim(used, col_index % ratio * cols_here, cols_here, 1)
    col_panel = spread(piece, "row", col_index // ratio)
    product = jnp.einsum(
        "ij,sjw->siw", inverse_block, col_panel.astype(jnp.float32), precision=lax.Precision.HIGHEST
    )
    term = -(product * row_mask[:, :, None].astype(jnp.float32))
    inverse_panel = lax.psum_scatter(term, "col", scatter_dimension=1, tiled=True)
    own_rows = lax.dynamic_slice_in_dim(used, col_index * span, span, 1).astype(jnp.float32)
    partial_update = jnp.einsum(
        "siv,siw->svw", own_rows, inverse_panel, precision=lax.Precision.HIGHEST
    )
    scattered = lax.psum_scatter(partial_update, "col", scatter_dimension=1, tiled=True)
    update = -lax.psum(scattered, "row")
    return (inverse_panel, update)


def solution(mesh):
    return jax.shard_map(
        shards,
        mesh=mesh,
        in_specs=(P("row", "col"), P(None, "row", None), P()),
        out_specs=(P(None, ("row", "col"), None), P(None, "col", None)),
        check_vma=False,
    )
```

profile of v0, /device:TPU:1, one launch (start us, length us, event | category | flops | bytes accessed | tf_op | source)
XLA Modules:
  0.0 639.9 jit_solution(3421007438243444268)
XLA Ops:
  7.2 0.0 copy-start
  7.2 0.0 all-reduce.5.cloned.1.call-start
  7.3 0.8 select_reduce_fusion
  8.1 1.5 copy.14
  9.6 0.1 broadcast_multiply_fusion
  9.7 1.0 copy-done.1
  10.7 0.9 dynamic-slice_select_fusion
  11.6 0.0 all-reduce.5.cloned.1.call-update
  11.6 0.0 all-reduce.9.cloned.1.call-start
  11.6 121.4 %all-reduce.5.cloned.1.call-done = bf16[2,256,512]{1,2,0:T(8,128)(2,1)} async-done(((bf16[2,256,512]{1,2,0:T(8,128)(2,1)}), bf16[2,256,512]{1,2,0:T(8,128)(2,1)}) %all-reduce.5.cloned.1.call-update) | async-done | bytes 524304 | tf_op jit(solution)/shard_map/psum | solution.py:11
  133.1 2.2 negate_bitcast_fusion
  135.2 2.4 copy.15
  137.7 0.0 all-reduce.9.cloned.1.call-update
  137.7 0.0 reduce-scatter.2.cloned.1.call-start
  137.8 1.3 dynamic-slice
  139.7 159.3 %all-reduce.9.cloned.1.call-done = f32[2,512,512]{2,0,1:T(2,128)} async-done(((f32[2,512,512]{2,0,1:T(2,128)}), f32[2,512,512]{2,0,1:T(2,128)}) %all-reduce.9.cloned.1.call-update) | async-done | bytes 2097168
  299.0 0.8 constant_dynamic-slice_fusion
  299.9 3.3 fusion.1
  303.2 0.0 reduce-scatter.2.cloned.1.call-update
  303.2 0.0 all-reduce.7.cloned.1.call-start
  303.3 217.5 %reduce-scatter.2.cloned.1.call-done = f32[2,16,512]{2,1,0:T(8,128)} async-done(((f32[2,512,512]{2,1,0:T(8,128)}), f32[2,16,512]{2,1,0:T(8,128)}) %reduce-scatter.2.cloned.1.call-update) | async-done | bytes 65552 | tf_op jit(solution)/shard_map/reduce_scatter | solution.py:39
  520.8 0.0 all-reduce.7.cloned.1.call-update
  520.8 111.0 %all-reduce.7.cloned.1.call-done = f32[2,16,512]{2,1,0:T(8,128)} async-done(((f32[2,16,512]{2,1,0:T(8,128)}), f32[2,16,512]{2,1,0:T(8,128)}) %all-reduce.7.cloned.1.call-update) | async-done | bytes 65552 | tf_op jit(solution)/shard_map/psum | solution.py:40
  631.8 1.5 neg.11
  (8 shorter events, 0.1 us)
Async XLA Ops:
  7.2 125.9 %copy-start = (f32[512,256]{1,0:T(8,128)S(1)}, f32[512,256]{1,0:T(8,128)}, u32[]{:S(2)}) copy-start(f32[512,256]{1,0:T(8,128)} %param.3) | copy-start | bytes 1572868
  7.2 125.9 %all-reduce.5.cloned.1.call-start = ((), (), s32[]{:S(2)}) async-start(), calls=%async_computation.1 | async-start | bytes 1048576 | tf_op jit(solution)/shard_map/psum | solution.py:11
  9.7 1.0 copy-start.1
  11.6 287.4 %all-reduce.9.cloned.1.call-start = ((), (), s32[]{:S(2)}) async-start(), calls=%async_computation.4 | async-start | bytes 4194304
  137.7 383.1 %reduce-scatter.2.cloned.1.call-start = ((), (), s32[]{:S(2)}) async-start(), calls=%async_computation.2 | async-start | bytes 2162688 | tf_op jit(solution)/shard_map/reduce_scatter | solution.py:39
  299.9 3.4 copy-start.2
  303.2 328.6 %all-reduce.7.cloned.1.call-start = ((), (), s32[]{:S(2)}) async-start(), calls=%async_computation.3 | async-start | bytes 131072 | tf_op jit(solution)/shard_map/psum | solution.py:40
Sparse Core Ops, SparseCore 0:
  11.7 121.3 all-reduce.4
  137.8 161.1 all-reduce.8
  303.4 217.3 reduce-scatter.1
  523.1 108.7 all-reduce.6
where the time goes:
time: 640 us
  waiting for transfers between devices  609 us (95%)
  between operations  14.5 us (2%)
  local copies, waits for them, and re-layouts  7.04 us (1%)
    reduce_scatter x1, waiting for transfers between devices, shards(): lax.psum_scatter(partial_update, 'col', scatter_dimension=1, tiled=True)  218 us
    unnamed x5, waiting for transfers between devices  159 us
    psum x1, waiting for transfers between devices, spread(): return lax.psum(block, axis)  121 us
    psum x1, waiting for transfers between devices, shards(): update = -lax.psum(scattered, 'row')  111 us
  transfers between devices with their start and end apart: 4, of which 4 were waited for; matrix products, arithmetic and copies ran while one was open for 0% of the time, Pallas kernels for 0%

commit v1 on v0

v1 whole, which is shorter than its diff:
```python
import functools

import jax
import jax.numpy as jnp
from jax import lax
from jax.experimental import pallas as pl
from jax.experimental.pallas import tpu as pltpu
from jax.sharding import PartitionSpec as P

MESH = pl.DeviceIdType.MESH
F32 = jnp.float32
BF16 = jnp.bfloat16
I16 = jnp.int16
NZ, NQ, NX, NY = 8, 2, 4, 8
TOP = 32767.0
TINY = 1e-30


def split(value):
    high = value.astype(BF16)
    return high, (value - high.astype(F32)).astype(BF16)


def kernel(
    pattern, a_hbm, panels_hbm, ip_out, up_out,
    a_v, u_v, lhs, pf, tb, pb, xb, zs, zsc, zr, zrsc, own, ipo, ub, ux, uo, ur, uf,
    in_sem, pf_send, pf_recv, xs_send, xs_recv, zs_send, zr_recv, zc_send, zc_recv,
    ip_send, ip_recv, ux_send, ux_recv, us_send, ur_recv, uf_send, uf_recv,
):
    row = lax.axis_index("row")
    col = lax.axis_index("col")
    z, q = row // 2, row % 2
    y, x = col // 4, col % 4

    def loads():
        yield pltpu.make_async_copy(a_hbm, a_v, in_sem.at[0])
        for p in range(4):
            yield pltpu.make_async_copy(
                panels_hbm.at[p // 2, :, pl.ds((p % 2) * 256, 256)], u_v.at[p], in_sem.at[1 + p]
            )

    for copy in loads():
        copy.start()

    pf_row, pf_col = y * 2 + x % 2, z * 4 + q * 2 + x // 2
    pf_self = jnp.logical_and(pf_row == row, pf_col == col)
    from_row, from_col = y * 2 + x // 2, z * 4 + (x % 2) * 2 + q
    ip_src_col, ip_src_core = row * 2 + col // 16, (col % 16) // 8
    ip_row = y * 2 + x // 2
    ip_col0 = (x % 2) * 16 + q * 8
    ip_has_self = jnp.logical_and(ip_row == row, jnp.logical_and(col >= ip_col0, col < ip_col0 + 8))

    barrier = pltpu.get_barrier_semaphore()

    @pl.loop(1, 16)
    def _(step):
        pl.semaphore_signal(barrier, inc=1, device_id=((row + step) % 16, col), device_id_type=MESH)

    @pl.loop(1, 32)
    def _(step):
        pl.semaphore_signal(barrier, inc=1, device_id=(row, (col + step) % 32), device_id_type=MESH)

    @pl.loop(0, 8)
    def _(step):
        source = step * 2 + ip_src_core

        @pl.when(jnp.logical_or(source != row, ip_src_col != col))
        def _():
            pl.semaphore_signal(barrier, inc=1, device_id=(source, ip_src_col), device_id_type=MESH)

    @pl.when(jnp.logical_not(pf_self))
    def _():
        pl.semaphore_signal(barrier, inc=1, device_id=(from_row, from_col), device_id_type=MESH)

    pl.semaphore_wait(
        barrier, 15 + 31 + 8 + 1 - ip_has_self.astype(jnp.int32) - pf_self.astype(jnp.int32)
    )

    pf_src = panels_hbm.at[y // 4, pl.ds(pl.multiple_of(x * 128, 128), 128), :]
    pf_copy = pltpu.make_async_remote_copy(
        src_ref=pf_src, dst_ref=pf, send_sem=pf_send, recv_sem=pf_recv,
        device_id=(pf_row, pf_col), device_id_type=MESH,
    )

    @pl.when(pf_self)
    def _():
        pltpu.make_async_copy(pf_src, pf, pf_recv).start()

    @pl.when(jnp.logical_not(pf_self))
    def _():
        pf_copy.start()

    copies = list(loads())
    copies[0].wait()
    high, low = split(a_v[...].T)
    lhs[0:256] = high
    lhs[256:512] = low
    for copy in copies[1:]:
        copy.wait()

    def exchange(p):
        return pltpu.make_async_remote_copy(
            src_ref=pb.at[1 - q, pl.ds(2 * p, 2)], dst_ref=xb.at[pl.ds(2 * p, 2)],
            send_sem=xs_send.at[p], recv_sem=xs_recv.at[p],
            device_id=(row + 1 - 2 * q, col), device_id_type=MESH,
        )

    pairs = [(z // 2 + step) % 4 for step in (2, 1, 3, 0)]
    for p in pairs:
        parts = []
        for b in range(4):
            keep = pattern[p // 2, row * 4 + b].astype(F32)
            parts.append(u_v[p, b * 128:(b + 1) * 128] * jnp.full((128, 256), keep, F32).astype(BF16))
        both = jnp.dot(lhs[...], jnp.concatenate(parts, 0), preferred_element_type=F32)
        product = both[0:256] + both[256:512]
        for half in range(2):
            for which in range(2):
                pb[half, 2 * p + which] = product[half * 128:(half + 1) * 128, which * 128:(which + 1) * 128]
        exchange(p).start()

    def to_z(d):
        return (
            pltpu.make_async_remote_copy(
                src_ref=zs.at[d], dst_ref=zr.at[z], send_sem=zs_send.at[d], recv_sem=zr_recv.at[z],
                device_id=(d * 2 + q, col), device_id_type=MESH,
            ),
            pltpu.make_async_remote_copy(
                src_ref=zsc.at[d], dst_ref=zrsc.at[z], send_sem=zc_send.at[d], recv_sem=zc_recv.at[z],
                device_id=(d * 2 + q, col), device_id_type=MESH,
            ),
        )

    for p in pairs:
        exchange(p).wait_recv()
        for which in range(2):
            d = 2 * p + which
            total = pb[q, d] + xb[d]

            @pl.when(d == z)
            def _():
                own[...] = total

            @pl.when(d != z)
            def _():
                top = jnp.maximum(jnp.max(jnp.abs(total), axis=0, keepdims=True), TINY)
                zs[d] = jnp.round(total * (TOP / top)).astype(jnp.int32).astype(I16)
                zsc[d] = jnp.broadcast_to(top * (1.0 / TOP), (8, 128))
                for copy in to_z(d):
                    copy.start()

    pltpu.make_async_copy(pf_src, pf, pf_recv).wait()
    flipped = pf[...].T
    tb[:, 0:128] = flipped
    tb[:, 128:256] = flipped

    for step in (7, 1, 6, 2, 5, 3, 4):
        source = (z + step) % 8
        pltpu.make_async_copy(zr.at[source], zr.at[source], zr_recv.at[source]).wait()
        pltpu.make_async_copy(zrsc.at[source], zrsc.at[source], zc_recv.at[source]).wait()
        own[...] += zr[source].astype(jnp.int32).astype(F32) * zrsc[source][0:1]
    mask = pattern[z // 4, 2 * col + q].astype(F32)
    block = own[...] * (-mask)
    ipo[...] = block

    ip_dst = ip_out.at[z // 4, :, pl.ds(pl.multiple_of((z % 4) * 128, 128), 128)]

    def to_owner(kk):
        return pltpu.make_async_remote_copy(
            src_ref=ipo.at[pl.ds(kk * 16, 16)], dst_ref=ip_dst, send_sem=ip_send.at[kk], recv_sem=ip_recv,
            device_id=(ip_row, ip_col0 + kk), device_id_type=MESH,
        )

    @pl.loop(0, 8)
    def _(kk):
        is_self = jnp.logical_and(ip_row == row, ip_col0 + kk == col)

        @pl.when(is_self)
        def _():
            pltpu.make_async_copy(ipo.at[pl.ds(kk * 16, 16)], ip_dst, ip_recv).start()

        @pl.when(jnp.logical_not(is_self))
        def _():
            to_owner(kk).start()

    high, low = split(block * mask)
    part = -jnp.dot(tb[...], jnp.concatenate([high, low], 0), preferred_element_type=F32)
    part = part.reshape(32, 2, 8, 128)
    for half in range(2):
        ub[half] = part[:, half]
    to_sibling = pltpu.make_async_remote_copy(
        src_ref=ub.at[1 - q], dst_ref=ux, send_sem=ux_send, recv_sem=ux_recv,
        device_id=(row + 1 - 2 * q, col), device_id_type=MESH,
    )
    to_sibling.start()
    to_sibling.wait_recv()
    uo[...] = ub[q] + ux[...]

    def to_col(step):
        there = (col + step) % 32
        return pltpu.make_async_remote_copy(
            src_ref=uo.at[there], dst_ref=ur.at[col], send_sem=us_send, recv_sem=ur_recv,
            device_id=(row, there), device_id_type=MESH,
        )

    @pl.loop(1, 32)
    def _(step):
        to_col(step).start()

    ur[col] = uo[col]
    arrived = ur.at[pl.ds(0, 31)]
    pltpu.make_async_copy(arrived, arrived, ur_recv).wait()
    uf[...] = jnp.sum(ur[...], axis=0)

    up_dst = up_out.at[
        z // 4, pl.ds(pl.multiple_of(q * 8, 8), 8), pl.ds(pl.multiple_of((z % 4) * 128, 128), 128)
    ]
    pltpu.make_async_copy(uf, up_dst, uf_recv).start()

    def to_row(step):
        return pltpu.make_async_remote_copy(
            src_ref=uf, dst_ref=up_dst, send_sem=uf_send.at[step], recv_sem=uf_recv,
            device_id=((row + step) % 16, col), device_id_type=MESH,
        )

    @pl.loop(1, 16)
    def _(step):
        to_row(step).start()

    @pl.when(jnp.logical_not(pf_self))
    def _():
        pf_copy.wait_send()

    for p in range(4):
        exchange(p).wait_send()

    @pl.loop(1, 8)
    def _(step):
        for copy in to_z((z + step) % 8):
            copy.wait_send()

    @pl.loop(0, 8)
    def _(kk):
        @pl.when(jnp.logical_or(ip_row != row, ip_col0 + kk != col))
        def _():
            to_owner(kk).wait_send()

    to_sibling.wait_send()
    pltpu.make_async_copy(arrived, arrived, us_send).wait()

    @pl.loop(1, 16)
    def _(step):
        to_row(step).wait_send()

    pltpu.make_async_copy(ip_out, ip_out, ip_recv).wait()
    pltpu.make_async_copy(up_out, up_out, uf_recv).wait()


def shards(inverse_block, panels, pattern):
    dma = pltpu.SemaphoreType.DMA
    return pl.pallas_call(
        kernel,
        out_shape=(
            jax.ShapeDtypeStruct((2, 16, 512), F32),
            jax.ShapeDtypeStruct((2, 16, 512), F32),
        ),
        in_specs=[
            pl.BlockSpec(memory_space=pltpu.SMEM),
            pl.BlockSpec(memory_space=pl.ANY),
            pl.BlockSpec(memory_space=pl.ANY),
        ],
        out_specs=(pl.BlockSpec(memory_space=pl.ANY), pl.BlockSpec(memory_space=pl.ANY)),
        scratch_shapes=[
            pltpu.VMEM((512, 256), F32),
            pltpu.VMEM((4, 512, 256), BF16),
            pltpu.VMEM((512, 512), BF16),
            pltpu.VMEM((128, 512), BF16),
            pltpu.VMEM((512, 256), BF16),
            pltpu.VMEM((2, 8, 128, 128), F32),
            pltpu.VMEM((8, 128, 128), F32),
            pltpu.VMEM((8, 128, 128), I16),
            pltpu.VMEM((8, 8, 128), F32),
            pltpu.VMEM((8, 128, 128), I16),
            pltpu.VMEM((8, 8, 128), F32),
            pltpu.VMEM((128, 128), F32),
            pltpu.VMEM((128, 128), F32),
            pltpu.VMEM((2, 32, 8, 128), F32),
            pltpu.VMEM((32, 8, 128), F32),
            pltpu.VMEM((32, 8, 128), F32),
            pltpu.VMEM((32, 8, 128), F32),
            pltpu.VMEM((8, 128), F32),
            dma((5,)), dma, dma, dma((4,)), dma((4,)), dma((8,)), dma((8,)), dma((8,)), dma((8,)),
            dma((8,)), dma, dma, dma, dma, dma, dma((16,)), dma,
        ],
        compiler_params=pltpu.CompilerParams(
            collective_id=0, has_side_effects=True, vmem_limit_bytes=32 * 1024 * 1024
        ),
        cost_estimate=pl.CostEstimate(flops=2 ** 29, bytes_accessed=2 ** 21, transcendentals=0),
    )(pattern, inverse_block, panels)


def solution(mesh):
    return jax.shard_map(
        shards,
        mesh=mesh,
        in_specs=(P("row", "col"), P(None, "row", None), P()),
        out_specs=(P(None, ("row", "col"), None), P(None, "col", None)),
        check_vma=False,
    )
```

time: 640 us -> 55.4 us (0.09)
  waiting for transfers between devices: 609 us -> 0 us
  Pallas kernels: 0 us -> 50.3 us
  between operations: 14.5 us -> 0.65 us
    psum x2 -> x0, waiting for transfers between devices: 232 us -> none  [the longest x1 121 us: spread(): return lax.psum(block, axis)]
    reduce_scatter x1 -> x0, waiting for transfers between devices: 218 us -> none  [shards(): lax.psum_scatter(partial_update, 'col', scatter_dimension=1, tiled=True)]
    unnamed x5 -> x0, waiting for transfers between devices: 159 us -> none
    pallas_call x0 -> x1, Pallas kernels: none -> 50.3 us  [shards(): pl.pallas_call(kernel, out_shape=(jax.ShapeDtypeStruct((2, 16, 512), F32)...]
  transfers between devices with their start and end apart: 4 -> 0, of which waited for: 4 -> 0; matrix products, arithmetic and copies ran while one was open for 0% -> 0% of each run, Pallas kernels for 0% -> 0%
where the time goes in v1:
time: 55.4 us; the launch traced here: 55.2 us
  Pallas kernels  50.3 us (91%)
  local copies, waits for them, and re-layouts  4.2 us (8%)
  between operations  0.65 us (1%)
    pallas_call x1, Pallas kernels, shards(): pl.pallas_call(kernel, out_shape=(jax.ShapeDtypeStruct((2, 16, 512), F32)...  50.3 us
    unnamed x8, local copies, waits for them, and re-layouts  4.2 us

profile of v1, /device:TPU:1, one launch (start us, length us, event | category | flops | bytes accessed | tf_op | source)
XLA Modules:
  0.0 55.2 jit_solution(973981895389755835)
XLA Ops:
  0.6 0.0 copy-start
  0.6 1.2 %copy-done = bf16[2,512,512]{2,1,0:T(8,128)(2,1)S(1)} copy-done((bf16[2,512,512]{2,1,0:T(8,128)(2,1)S(1)}, bf16[2,512,512]{2,1,0:T(8,128)(2,1)}, u32[]{:S(2)}) %copy-start) | copy-done | bytes 1048600
  1.9 0.0 copy-start.1
  1.9 1.0 %copy-done.1 = f32[512,256]{1,0:T(8,128)S(1)} copy-done((f32[512,256]{1,0:T(8,128)S(1)}, f32[512,256]{1,0:T(8,128)}, u32[]{:S(2)}) %copy-start.1) | copy-done | bytes 524312
  2.9 0.0 copy-start.2
  2.9 0.7 %copy-done.2 = s32[2,64]{1,0:T(2,128)S(1)} copy-done((s32[2,64]{1,0:T(2,128)S(1)}, s32[2,64]{1,0:T(2,128)}, u32[]{:S(2)}) %copy-start.2) | copy-done | bytes 536
  3.6 50.3 %shard_map.50 = (f32[2,16,512]{2,1,0:T(8,128)S(1)}, f32[2,16,512]{2,1,0:T(8,128)S(1)}) custom-call(s32[2,64]{1,0:T(2,128)S(1)} %copy-done.2, f32[512,256]{1,0:T(8,128)S(1)} %copy-done.1, bf16[2,512,512]{2,1,0:T(8,128)(2,1)S(1)} %copy-done), custom_call_target="tpu_custom_call" | custom-call | flops 536870912 | bytes 2097152 | tf_op jit(solution)/shard_map/pallas_call | solution.py:260
  53.9 0.6 %copy.7 = f32[2,16,512]{2,1,0:T(8,128)} copy(f32[2,16,512]{2,1,0:T(8,128)S(1)} %get-tuple-element.4) | data formatting | bytes 131072
  54.5 0.6 %copy.8 = f32[2,16,512]{2,1,0:T(8,128)} copy(f32[2,16,512]{2,1,0:T(8,128)S(1)} %get-tuple-element.5) | data formatting | bytes 131072
Async XLA Ops:
  0.6 1.2 %copy-start = (bf16[2,512,512]{2,1,0:T(8,128)(2,1)S(1)}, bf16[2,512,512]{2,1,0:T(8,128)(2,1)}, u32[]{:S(2)}) copy-start(bf16[2,512,512]{2,1,0:T(8,128)(2,1)} %panels_hbm.1) | copy-start | bytes 3145732
  1.9 1.0 %copy-start.1 = (f32[512,256]{1,0:T(8,128)S(1)}, f32[512,256]{1,0:T(8,128)}, u32[]{:S(2)}) copy-start(f32[512,256]{1,0:T(8,128)} %a_hbm.1) | copy-start | bytes 1572868
  2.9 0.7 %copy-start.2 = (s32[2,64]{1,0:T(2,128)S(1)}, s32[2,64]{1,0:T(2,128)}, u32[]{:S(2)}) copy-start(s32[2,64]{1,0:T(2,128)} %pattern.1) | copy-start | bytes 1540

commit v2 on v1

v2 whole, which is shorter than its diff:
```python
import functools

import jax
import jax.numpy as jnp
from jax import lax
from jax.experimental import pallas as pl
from jax.experimental.pallas import tpu as pltpu
from jax.sharding import PartitionSpec as P

MESH = pl.DeviceIdType.MESH
F32 = jnp.float32
BF16 = jnp.bfloat16
I16 = jnp.int16
NZ, NQ, NX, NY = 8, 2, 4, 8
TOP = 32767.0
TINY = 1e-30


def split(value):
    high = value.astype(BF16)
    return high, (value - high.astype(F32)).astype(BF16)


def kernel(
    pattern, a_hbm, panels_hbm, ip_out, up_out,
    a_v, u_v, lhs, pm, pf, tb, pb, xb, zs, zsc, zr, zrsc, own, ipo, im, ub, ux, uo, ur, uf,
    in_sem, pm_send, pm_recv, pf_send, pf_recv, xs_send, xs_recv, zs_send, zr_recv, zc_send, zc_recv,
    im_send, im_recv, ip_send, ip_recv, ux_send, ux_recv, us_send, ur_recv, uf_send, uf_recv,
):
    row = lax.axis_index("row")
    col = lax.axis_index("col")
    z, q = row // 2, row % 2
    y, x = col // 4, col % 4
    sibling = (row + 1 - 2 * q, col)

    def remote(src, dst, send, recv, there):
        return pltpu.make_async_remote_copy(
            src_ref=src, dst_ref=dst, send_sem=send, recv_sem=recv, device_id=there, device_id_type=MESH
        )

    def arrival(ref, sem):
        return pltpu.make_async_copy(ref, ref, sem)

    def start(here, src, dst, send, recv, there):
        @pl.when(here)
        def _():
            pltpu.make_async_copy(src, dst, recv).start()

        @pl.when(jnp.logical_not(here))
        def _():
            remote(src, dst, send, recv, there).start()

    def sent(here, src, dst, send, recv, there):
        @pl.when(jnp.logical_not(here))
        def _():
            remote(src, dst, send, recv, there).wait_send()

    def far_first(step, count):
        half = (step + 1) // 2
        return count // 2 + jnp.where(step % 2 == 0, half, -half)

    pairs = [(z // 2 + step) % 4 for step in (2, 1, 3, 0)]

    def load_u(p):
        return pltpu.make_async_copy(
            panels_hbm.at[p // 2, :, pl.ds(pl.multiple_of((p % 2) * 256, 256), 256)], u_v.at[p], in_sem.at[1 + p]
        )

    load_a = pltpu.make_async_copy(a_hbm, a_v, in_sem.at[0])
    load_a.start()
    for p in pairs:
        load_u(p).start()

    barrier = pltpu.get_barrier_semaphore()

    @pl.loop(0, 31)
    def _(step):
        there = (row, (col + far_first(step, 32)) % 32)
        pl.semaphore_signal(barrier, inc=1, device_id=there, device_id_type=MESH)

    @pl.loop(0, 15)
    def _(step):
        there = ((row + far_first(step, 16)) % 16, col)
        pl.semaphore_signal(barrier, inc=1, device_id=there, device_id_type=MESH)

    load_a.wait()
    high, low = split(a_v[...].T)
    lhs[0:256] = high
    lhs[256:512] = low
    for p in pairs:
        load_u(p).wait()
        parts = []
        for b in range(4):
            keep = pattern[p // 2, row * 4 + b].astype(F32)
            parts.append(u_v[p, b * 128:(b + 1) * 128] * jnp.full((128, 256), keep, F32).astype(BF16))
        both = jnp.dot(lhs[...], jnp.concatenate(parts, 0), preferred_element_type=F32)
        product = both[0:256] + both[256:512]
        for half in range(2):
            for which in range(2):
                pb[half, 2 * p + which] = product[half * 128:(half + 1) * 128, which * 128:(which + 1) * 128]

    pl.semaphore_wait(barrier, 46)

    pm_z, pm_q = (16 - y - z) % 8, x % 2
    pm_args = (
        jnp.logical_and(pm_z == z, pm_q == q),
        panels_hbm.at[pm_z // 4, pl.ds(pl.multiple_of(x * 128, 128), 128), :], pm.at[q],
        pm_send, pm_recv.at[q], (pm_z * 2 + pm_q, col),
    )
    start(*pm_args)

    def exchange(p):
        return remote(
            pb.at[1 - q, pl.ds(2 * p, 2)], xb.at[pl.ds(2 * p, 2)], xs_send.at[p], xs_recv.at[p], sibling
        )

    for p in pairs:
        exchange(p).start()

    def to_z(d):
        there = (d * 2 + q, col)
        return (
            remote(zs.at[d], zr.at[z], zs_send.at[d], zr_recv.at[z], there),
            remote(zsc.at[d], zrsc.at[z], zc_send.at[d], zc_recv.at[z], there),
        )

    for p in pairs:
        exchange(p).wait_recv()
        for which in range(2):
            d = 2 * p + which
            total = pb[q, d] + xb[d]

            @pl.when(d == z)
            def _():
                own[...] = total

            @pl.when(d != z)
            def _():
                top = jnp.maximum(jnp.max(jnp.abs(total), axis=0, keepdims=True), TINY)
                zs[d] = jnp.round(total * (TOP / top)).astype(jnp.int32).astype(I16)
                zsc[d] = jnp.broadcast_to(top * (1.0 / TOP), (8, 128))
                for copy in to_z(d):
                    copy.start()

    def pf_args(core):
        there_x, there_y = core * 2 + x // 2, pm_z
        return (
            jnp.logical_and(there_x == x, there_y == y),
            pm.at[core], pf, pf_send.at[core], pf_recv, (row, there_y * 4 + there_x),
        )

    forwards_pf = x % 2 == q

    @pl.when(forwards_pf)
    def _():
        for core in range(2):
            arrival(pm.at[core], pm_recv.at[core]).wait()
            start(*pf_args(core))

    arrival(pf, pf_recv).wait()
    flipped = pf[...].T
    tb[:, 0:128] = flipped
    tb[:, 128:256] = flipped

    for step in (7, 1, 6, 2, 5, 3, 4):
        source = (z + step) % 8
        arrival(zr.at[source], zr_recv.at[source]).wait()
        arrival(zrsc.at[source], zc_recv.at[source]).wait()
        own[...] += zr[source].astype(jnp.int32).astype(F32) * zrsc[source][0:1]
    mask = pattern[z // 4, 2 * col + q].astype(F32)
    block = own[...] * (-mask)
    ipo[...] = block

    def im_args(kk):
        there_x, there_y = kk % 4, (x % 2) * 4 + q * 2 + kk // 4
        return (
            jnp.logical_and(there_x == x, there_y == y),
            ipo.at[pl.ds(pl.multiple_of(kk * 16, 16), 16)], im.at[y * 2 + x // 2], im_send.at[kk], im_recv,
            (row, there_y * 4 + there_x),
        )

    @pl.loop(0, 8)
    def _(kk):
        start(*im_args(kk))

    high, low = split(block * mask)
    part = -jnp.dot(tb[...], jnp.concatenate([high, low], 0), preferred_element_type=F32)
    part = part.reshape(32, 2, 8, 128)
    for half in range(2):
        ub[half] = part[:, half]
    to_sibling = remote(ub.at[1 - q], ux, ux_send, ux_recv, sibling)
    to_sibling.start()
    to_sibling.wait_recv()
    uo[...] = ub[q] + ux[...]

    def to_col(step):
        there = (col + far_first(step, 32)) % 32
        return remote(uo.at[there], ur.at[col], us_send, ur_recv, (row, there))

    @pl.loop(0, 31)
    def _(step):
        to_col(step).start()

    ur[col] = uo[col]

    def ip_args(there):
        return (
            there == row,
            im.at[there], ip_out.at[z // 4, :, pl.ds(pl.multiple_of((z % 4) * 128, 128), 128)],
            ip_send.at[there], ip_recv, (there, col),
        )

    forwards_ip = (y % 4) // 2 == q

    @pl.when(forwards_ip)
    def _():
        arrival(im, im_recv).wait()

        @pl.loop(0, 16)
        def _(step):
            start(*ip_args((row + 8 + step) % 16))

    arrived = ur.at[pl.ds(0, 31)]
    arrival(arrived, ur_recv).wait()
    uf[...] = jnp.sum(ur[...], axis=0)

    up_dst = up_out.at[
        z // 4, pl.ds(pl.multiple_of(q * 8, 8), 8), pl.ds(pl.multiple_of((z % 4) * 128, 128), 128)
    ]

    def to_row(step):
        return remote(uf, up_dst, uf_send.at[step], uf_recv, ((row + far_first(step, 16)) % 16, col))

    @pl.loop(0, 15)
    def _(step):
        to_row(step).start()

    pltpu.make_async_copy(uf, up_dst, uf_recv).start()

    sent(*pm_args)

    @pl.when(forwards_pf)
    def _():
        for core in range(2):
            sent(*pf_args(core))

    for p in range(4):
        exchange(p).wait_send()

    @pl.loop(1, 8)
    def _(step):
        for copy in to_z((z + step) % 8):
            copy.wait_send()

    @pl.loop(0, 8)
    def _(kk):
        sent(*im_args(kk))

    to_sibling.wait_send()
    arrival(arrived, us_send).wait()

    @pl.when(forwards_ip)
    def _():
        @pl.loop(0, 16)
        def _(there):
            sent(*ip_args(there))

    @pl.loop(0, 15)
    def _(step):
        to_row(step).wait_send()

    arrival(ip_out, ip_recv).wait()
    arrival(up_out, uf_recv).wait()


def shards(inverse_block, panels, pattern):
    dma = pltpu.SemaphoreType.DMA
    return pl.pallas_call(
        kernel,
        out_shape=(
            jax.ShapeDtypeStruct((2, 16, 512), F32),
            jax.ShapeDtypeStruct((2, 16, 512), F32),
        ),
        in_specs=[
            pl.BlockSpec(memory_space=pltpu.SMEM),
            pl.BlockSpec(memory_space=pl.ANY),
            pl.BlockSpec(memory_space=pl.ANY),
        ],
        out_specs=(pl.BlockSpec(memory_space=pl.ANY), pl.BlockSpec(memory_space=pl.ANY)),
        scratch_shapes=[
            pltpu.VMEM((512, 256), F32),
            pltpu.VMEM((4, 512, 256), BF16),
            pltpu.VMEM((512, 512), BF16),
            pltpu.VMEM((2, 128, 512), BF16),
            pltpu.VMEM((128, 512), BF16),
            pltpu.VMEM((512, 256), BF16),
            pltpu.VMEM((2, 8, 128, 128), F32),
            pltpu.VMEM((8, 128, 128), F32),
            pltpu.VMEM((8, 128, 128), I16),
            pltpu.VMEM((8, 8, 128), F32),
            pltpu.VMEM((8, 128, 128), I16),
            pltpu.VMEM((8, 8, 128), F32),
            pltpu.VMEM((128, 128), F32),
            pltpu.VMEM((128, 128), F32),
            pltpu.VMEM((16, 16, 128), F32),
            pltpu.VMEM((2, 32, 8, 128), F32),
            pltpu.VMEM((32, 8, 128), F32),
            pltpu.VMEM((32, 8, 128), F32),
            pltpu.VMEM((32, 8, 128), F32),
            pltpu.VMEM((8, 128), F32),
            dma((5,)), dma, dma((2,)), dma((2,)), dma, dma((4,)), dma((4,)), dma((8,)), dma((8,)), dma((8,)), dma((8,)),
            dma((8,)), dma, dma((16,)), dma, dma, dma, dma, dma, dma((16,)), dma,
        ],
        compiler_params=pltpu.CompilerParams(
            collective_id=0, has_side_effects=True, vmem_limit_bytes=60 * 1024 * 1024
        ),
        cost_estimate=pl.CostEstimate(flops=2 ** 29, bytes_accessed=2 ** 21, transcendentals=0),
    )(pattern, inverse_block, panels)


def solution(mesh):
    return jax.shard_map(
        shards,
        mesh=mesh,
        in_specs=(P("row", "col"), P(None, "row", None), P()),
        out_specs=(P(None, ("row", "col"), None), P(None, "col", None)),
        check_vma=False,
    )
```

time: 55.4 us -> 55.7 us (level)
  Pallas kernels: 50.3 us -> 52.7 us
  local copies, waits for them, and re-layouts: 4.2 us -> 2.14 us
    pallas_call x1, Pallas kernels: 50.3 us -> 52.7 us  [shards(): pl.pallas_call(kernel, out_shape=(jax.ShapeDtypeStruct((2, 16, 512), F32)...]
    unnamed x8 -> x4, local copies, waits for them, and re-layouts: 4.2 us -> 2.14 us
where the time goes in v2:
time: 55.7 us; the launch traced here: 55.5 us
  Pallas kernels  52.7 us (95%)
  local copies, waits for them, and re-layouts  2.14 us (4%)
  between operations  0.65 us (1%)
    pallas_call x1, Pallas kernels, shards(): pl.pallas_call(kernel, out_shape=(jax.ShapeDtypeStruct((2, 16, 512), F32)...  52.7 us
    unnamed x4, local copies, waits for them, and re-layouts  2.14 us

profile of v2, /device:TPU:1, one launch (start us, length us, event | category | flops | bytes accessed | tf_op | source)
XLA Modules:
  0.0 55.5 jit_solution(6098344295599109039)
XLA Ops:
  0.6 52.7 %shard_map.50 = (f32[2,16,512]{2,1,0:T(8,128)}, f32[2,16,512]{2,1,0:T(8,128)}) custom-call(s32[2,64]{1,0:T(2,128)} %pattern.1, f32[512,256]{1,0:T(8,128)} %a_hbm.1, bf16[2,512,512]{2,1,0:T(8,128)(2,1)} %panels_hbm.1), custom_call_target="tpu_custom_call" | custom-call | flops 536870912 | bytes 2097152 | tf_op jit(solution)/shard_map/pallas_call | solution.py:278
  53.3 0.0 copy-start
  53.3 1.5 %copy.7 = f32[2,16,512]{2,1,0:T(8,128)} copy(f32[2,16,512]{2,1,0:T(8,128)} %get-tuple-element.4) | data formatting | bytes 131072
  54.8 0.0 copy-done
  54.8 0.6 %copy.8 = f32[2,16,512]{2,1,0:T(8,128)} copy(f32[2,16,512]{2,1,0:T(8,128)S(1)} %copy-done) | data formatting | bytes 131072
Async XLA Ops:
  53.3 1.5 %copy-start = (f32[2,16,512]{2,1,0:T(8,128)S(1)}, f32[2,16,512]{2,1,0:T(8,128)}, u32[]{:S(2)}) copy-start(f32[2,16,512]{2,1,0:T(8,128)} %get-tuple-element.5) | copy-start | bytes 196612

commit v3 on v2

v3 whole, which is shorter than its diff:
```python
import functools

import jax
import jax.numpy as jnp
from jax import lax
from jax.experimental import pallas as pl
from jax.experimental.pallas import tpu as pltpu
from jax.sharding import PartitionSpec as P

MESH = pl.DeviceIdType.MESH
F32 = jnp.float32
BF16 = jnp.bfloat16
I16 = jnp.int16
NZ, NQ, NX, NY = 8, 2, 4, 8
TOP = 32767.0
TINY = 1e-30


def split(value):
    high = value.astype(BF16)
    return high, (value - high.astype(F32)).astype(BF16)


def kernel(
    pattern, a_hbm, panels_hbm, ip_out, up_out,
    a_v, u_v, lhs, pm, pf, tb, pb, xb, zs, zsc, zr, zrsc, own, im, ub, ux, uo, ur, uf, ipo, up_all,
    in_sem, pm_send, pm_recv, pf_send, pf_recv, xs_send, xs_recv, zs_send, zr_recv, zc_send, zc_recv,
    im_send, im_recv, ip_send, ip_recv, ux_send, ux_recv, us_send, ur_recv, uf_send, uf_recv,
):
    row = lax.axis_index("row")
    col = lax.axis_index("col")
    z, q = row // 2, row % 2
    y, x = col // 4, col % 4
    sibling = (row + 1 - 2 * q, col)

    def remote(src, dst, send, recv, there):
        return pltpu.make_async_remote_copy(
            src_ref=src, dst_ref=dst, send_sem=send, recv_sem=recv, device_id=there, device_id_type=MESH
        )

    def arrival(ref, sem):
        return pltpu.make_async_copy(ref, ref, sem)

    def start(here, src, dst, send, recv, there):
        @pl.when(here)
        def _():
            pltpu.make_async_copy(src, dst, recv).start()

        @pl.when(jnp.logical_not(here))
        def _():
            remote(src, dst, send, recv, there).start()

    def sent(here, src, dst, send, recv, there):
        @pl.when(jnp.logical_not(here))
        def _():
            remote(src, dst, send, recv, there).wait_send()

    def far_first(step, count):
        half = (step + 1) // 2
        return count // 2 + jnp.where(step % 2 == 0, half, -half)

    def pair(step):
        return (z // 2 + jnp.where(step == 0, 2, jnp.where(step == 3, 0, 2 * step - 1))) % 4

    def load_u(p):
        return pltpu.make_async_copy(
            panels_hbm.at[p // 2, :, pl.ds(pl.multiple_of((p % 2) * 256, 256), 256)], u_v.at[p], in_sem.at[1 + p]
        )

    load_a = pltpu.make_async_copy(a_hbm, a_v, in_sem.at[0])
    load_a.start()
    for step in range(4):
        load_u(pair(step)).start()

    barrier = pltpu.get_barrier_semaphore()

    @pl.loop(0, 31)
    def _(step):
        there = (row, (col + far_first(step, 32)) % 32)
        pl.semaphore_signal(barrier, inc=1, device_id=there, device_id_type=MESH)

    @pl.loop(0, 15)
    def _(step):
        there = ((row + far_first(step, 16)) % 16, col)
        pl.semaphore_signal(barrier, inc=1, device_id=there, device_id_type=MESH)

    load_a.wait()
    high, low = split(a_v[...].T)
    lhs[0:256] = high
    lhs[256:512] = low

    @pl.loop(0, 4)
    def _(step):
        p = pair(step)
        load_u(p).wait()
        parts = []
        for b in range(4):
            keep = pattern[p // 2, row * 4 + b].astype(F32)
            parts.append(u_v[p, b * 128:(b + 1) * 128] * jnp.full((128, 256), keep, F32).astype(BF16))
        both = jnp.dot(lhs[...], jnp.concatenate(parts, 0), preferred_element_type=F32)
        product = both[0:256] + both[256:512]
        for half in range(2):
            for which in range(2):
                first = which * 128 + half * 64
                pb[half, 2 * p + which] = product[first:first + 64]

    pl.semaphore_wait(barrier, 46)

    pm_z = (2 * z + 12 - y) % 8
    pm_slot = ((y + 9 - z) % 8) // 4
    sends_pm = q == x // 2
    hands_on = (y + z) % 2 == 0

    def pm_args(core):
        first = (x % 2) * 256 + (pm_z % 2) * 128 + core * 64
        return (
            jnp.logical_and(pm_z == z, q == core),
            panels_hbm.at[pm_z // 4, pl.ds(pl.multiple_of(first, 64), 64), :], pm.at[pm_slot],
            pm_send.at[core], pm_recv.at[pm_slot], (pm_z * 2 + core, col),
        )

    def pf_args(turn):
        via = ((y + z) // 2 + 2 + 4 * turn) % 8
        slot = ((y + 9 - via) % 8) // 4
        return slot, (via == y, pm.at[slot], pf, pf_send.at[slot], pf_recv, (row, via * 4 + x))

    @pl.when(sends_pm)
    def _():
        for core in range(2):
            start(*pm_args(core))

    def exchange(p):
        return remote(
            pb.at[1 - q, pl.ds(2 * p, 2)], xb.at[pl.ds(2 * p, 2)], xs_send.at[p], xs_recv.at[p], sibling
        )

    for step in range(4):
        exchange(pair(step)).start()

    def to_z(d):
        there = (d * 2 + q, col)
        return (
            remote(zs.at[d], zr.at[z], zs_send.at[d], zr_recv.at[z], there),
            remote(zsc.at[d], zrsc.at[z], zc_send.at[d], zc_recv.at[z], there),
        )

    @pl.loop(0, 8)
    def _(step):
        p, which = pair(step // 2), step % 2
        d = 2 * p + which

        @pl.when(which == 0)
        def _():
            exchange(p).wait_recv()

        total = pb[q, d] + xb[d]

        @pl.when(d == z)
        def _():
            own[...] = total

        @pl.when(d != z)
        def _():
            top = jnp.maximum(jnp.max(jnp.abs(total), axis=0, keepdims=True), TINY)
            zs[d] = jnp.round(total * (TOP / top)).astype(jnp.int32).astype(I16)
            zsc[d] = top * (1.0 / TOP)
            for copy in to_z(d):
                copy.start()

    @pl.when(hands_on)
    def _():
        for turn in range(2):
            slot, args = pf_args(turn)
            arrival(pm.at[slot], pm_recv.at[slot]).wait()
            start(*args)

    arrival(pf, pf_recv).wait()
    flipped = pf[...].T
    tb[:, 0:64] = flipped
    tb[:, 64:128] = flipped

    @pl.loop(0, 7)
    def _(step):
        source = (z + far_first(6 - step, 8)) % 8
        arrival(zr.at[source], zr_recv.at[source]).wait()
        arrival(zrsc.at[source], zc_recv.at[source]).wait()
        own[...] += zr[source].astype(jnp.int32).astype(F32) * zrsc[source]
    mask = pattern[z // 4, 2 * col + z % 2].astype(F32)
    block = own[...] * (-mask)
    ipo[...] = block

    def im_args(kk):
        there_x, there_y = kk, (x % 2) * 4 + (z % 2) * 2 + q
        return (
            jnp.logical_and(there_x == x, there_y == y),
            ipo.at[pl.ds(pl.multiple_of(kk * 16, 16), 16)], im.at[y * 2 + x // 2], im_send.at[kk], im_recv,
            (row, there_y * 4 + there_x),
        )

    @pl.loop(0, 4)
    def _(kk):
        start(*im_args(kk))

    high, low = split(block * mask)
    part = -jnp.dot(tb[...], jnp.concatenate([high, low], 0), preferred_element_type=F32)
    for half in range(2):
        ub[half] = part[:, half * 128:(half + 1) * 128].reshape(32, 16, 128)
    to_sibling = remote(ub.at[1 - q], ux, ux_send, ux_recv, sibling)
    to_sibling.start()
    to_sibling.wait_recv()
    uo[...] = ub[q] + ux[...]

    def to_col(step):
        there = (col + far_first(step, 32)) % 32
        return remote(uo.at[there], ur.at[col], us_send, ur_recv, (row, there))

    @pl.loop(0, 31)
    def _(step):
        to_col(step).start()

    ur[col] = uo[col]

    def ip_args(there):
        return (
            there == row,
            im.at[there], ip_out.at[z // 4, :, pl.ds(pl.multiple_of((z // 2 % 2) * 256, 256), 256)],
            ip_send.at[there], ip_recv, (there, col),
        )

    forwards_ip = jnp.logical_and((y % 4) // 2 == z % 2, y % 2 == q)

    @pl.when(forwards_ip)
    def _():
        arrival(im, im_recv).wait()

        @pl.loop(0, 16)
        def _(step):
            start(*ip_args((row + 8 + step) % 16))

    arrived = ur.at[pl.ds(0, 31)]
    arrival(arrived, ur_recv).wait()
    uf[...] = jnp.sum(ur[...], axis=0)

    up_dst = up_all.at[row]

    def to_row(step):
        return remote(uf, up_dst, uf_send.at[step], uf_recv, ((row + far_first(step, 16)) % 16, col))

    @pl.loop(0, 15)
    def _(step):
        to_row(step).start()

    pltpu.make_async_copy(uf, up_dst, uf_recv).start()

    @pl.when(sends_pm)
    def _():
        for core in range(2):
            sent(*pm_args(core))

    @pl.when(hands_on)
    def _():
        for turn in range(2):
            sent(*pf_args(turn)[1])

    for p in range(4):
        exchange(p).wait_send()

    @pl.loop(1, 8)
    def _(step):
        for copy in to_z((z + step) % 8):
            copy.wait_send()

    @pl.loop(0, 4)
    def _(kk):
        sent(*im_args(kk))

    to_sibling.wait_send()
    arrival(arrived, us_send).wait()

    @pl.when(forwards_ip)
    def _():
        @pl.loop(0, 16)
        def _(there):
            sent(*ip_args(there))

    @pl.loop(0, 15)
    def _(step):
        to_row(step).wait_send()

    arrival(up_all, uf_recv).wait()
    for k in range(8):
        first = 4 * (k // 2) + k % 2
        up_out[k // 4, :, (k % 4) * 128:(k % 4 + 1) * 128] = up_all[first] + up_all[first + 2]
    arrival(ip_out, ip_recv).wait()


def shards(inverse_block, panels, pattern):
    dma = pltpu.SemaphoreType.DMA
    return pl.pallas_call(
        kernel,
        out_shape=(
            jax.ShapeDtypeStruct((2, 16, 512), F32),
            jax.ShapeDtypeStruct((2, 16, 512), F32),
        ),
        in_specs=[
            pl.BlockSpec(memory_space=pltpu.SMEM),
            pl.BlockSpec(memory_space=pl.ANY),
            pl.BlockSpec(memory_space=pl.ANY),
        ],
        out_specs=(pl.BlockSpec(memory_space=pl.ANY), pl.BlockSpec(memory_space=pltpu.VMEM)),
        scratch_shapes=[
            pltpu.VMEM((512, 256), F32),
            pltpu.VMEM((4, 512, 256), BF16),
            pltpu.VMEM((512, 512), BF16),
            pltpu.VMEM((2, 64, 512), BF16),
            pltpu.VMEM((64, 512), BF16),
            pltpu.VMEM((512, 128), BF16),
            pltpu.VMEM((2, 8, 64, 256), F32),
            pltpu.VMEM((8, 64, 256), F32),
            pltpu.VMEM((8, 64, 256), I16),
            pltpu.VMEM((8, 1, 256), F32),
            pltpu.VMEM((8, 64, 256), I16),
            pltpu.VMEM((8, 1, 256), F32),
            pltpu.VMEM((64, 256), F32),
            pltpu.VMEM((16, 16, 256), F32),
            pltpu.VMEM((2, 32, 16, 128), F32),
            pltpu.VMEM((32, 16, 128), F32),
            pltpu.VMEM((32, 16, 128), F32),
            pltpu.VMEM((32, 16, 128), F32),
            pltpu.VMEM((16, 128), F32),
            pltpu.VMEM((64, 256), F32),
            pltpu.VMEM((16, 16, 128), F32),
            dma((5,)), dma((2,)), dma((2,)), dma((2,)), dma, dma((4,)), dma((4,)), dma((8,)), dma((8,)), dma((8,)),
            dma((8,)), dma((4,)), dma, dma((16,)), dma, dma, dma, dma, dma, dma((16,)), dma,
        ],
        compiler_params=pltpu.CompilerParams(
            collective_id=0, has_side_effects=True, vmem_limit_bytes=60 * 1024 * 1024
        ),
        cost_estimate=pl.CostEstimate(flops=2 ** 29, bytes_accessed=2 ** 21, transcendentals=0),
    )(pattern, inverse_block, panels)


def solution(mesh):
    return jax.shard_map(
        shards,
        mesh=mesh,
        in_specs=(P("row", "col"), P(None, "row", None), P()),
        out_specs=(P(None, ("row", "col"), None), P(None, "col", None)),
        check_vma=False,
    )
```

time: 55.7 us -> 52.3 us (0.939)
  Pallas kernels: 52.7 us -> 49.3 us
    pallas_call x1, Pallas kernels: 52.7 us -> 49.3 us  [shards(): pl.pallas_call(kernel, out_shape=(jax.ShapeDtypeStruct((2, 16, 512), F32)...]
where the time goes in v3:
time: 52.3 us; the launch traced here: 52.1 us
  Pallas kernels  49.3 us (94%)
  local copies, waits for them, and re-layouts  2.14 us (4%)
  between operations  0.65 us (1%)
    pallas_call x1, Pallas kernels, shards(): pl.pallas_call(kernel, out_shape=(jax.ShapeDtypeStruct((2, 16, 512), F32)...  49.3 us
    unnamed x4, local copies, waits for them, and re-layouts  2.14 us

profile of v3, /device:TPU:1, one launch (start us, length us, event | category | flops | bytes accessed | tf_op | source)
XLA Modules:
  0.0 52.1 jit_solution(7482135548258692690)
XLA Ops:
  0.6 49.3 %shard_map.50 = (f32[2,16,512]{2,1,0:T(8,128)}, f32[2,16,512]{2,1,0:T(8,128)}) custom-call(s32[2,64]{1,0:T(2,128)} %pattern.1, f32[512,256]{1,0:T(8,128)} %a_hbm.1, bf16[2,512,512]{2,1,0:T(8,128)(2,1)} %panels_hbm.1), custom_call_target="tpu_custom_call" | custom-call | flops 536870912 | bytes 2097152 | tf_op jit(solution)/shard_map/pallas_call | solution.py:299
  50.0 0.0 copy-start
  50.0 1.5 %copy.7 = f32[2,16,512]{2,1,0:T(8,128)} copy(f32[2,16,512]{2,1,0:T(8,128)} %get-tuple-element.4) | data formatting | bytes 131072
  51.5 0.0 copy-done
  51.5 0.6 %copy.8 = f32[2,16,512]{2,1,0:T(8,128)} copy(f32[2,16,512]{2,1,0:T(8,128)S(1)} %copy-done) | data formatting | bytes 131072
Async XLA Ops:
  50.0 1.5 %copy-start = (f32[2,16,512]{2,1,0:T(8,128)S(1)}, f32[2,16,512]{2,1,0:T(8,128)}, u32[]{:S(2)}) copy-start(f32[2,16,512]{2,1,0:T(8,128)} %get-tuple-element.5) | copy-start | bytes 196612

commit v4 on v3

--- a/solution.py
+++ b/solution.py
@@ -22,10 +22,10 @@
 
 
 def kernel(
-    pattern, a_hbm, panels_hbm, ip_out, up_out,
-    a_v, u_v, lhs, pm, pf, tb, pb, xb, zs, zsc, zr, zrsc, own, im, ub, ux, uo, ur, uf, ipo, up_all,
+    pattern_hbm, a_hbm, panels_hbm, ip_out, up_out,
+    pattern, a_v, u_v, lhs, pm, pf, tb, pb, xb, zs, zsc, zr, zrsc, own, im, ub, ux, uq, usc, ur, ursc, uf, ipo, up_all, fin,
     in_sem, pm_send, pm_recv, pf_send, pf_recv, xs_send, xs_recv, zs_send, zr_recv, zc_send, zc_recv,
-    im_send, im_recv, ip_send, ip_recv, ux_send, ux_recv, us_send, ur_recv, uf_send, uf_recv,
+    im_send, im_recv, ip_send, ip_recv, ux_send, ux_recv, us_send, ur_recv, uc_send, uc_recv, uf_send, uf_recv, fin_send, fin_recv,
 ):
     row = lax.axis_index("row")
     col = lax.axis_index("col")
@@ -67,8 +67,10 @@
             panels_hbm.at[p // 2, :, pl.ds(pl.multiple_of((p % 2) * 256, 256), 256)], u_v.at[p], in_sem.at[1 + p]
         )
 
+    load_pattern = pltpu.make_async_copy(pattern_hbm, pattern, in_sem.at[5])
     load_a = pltpu.make_async_copy(a_hbm, a_v, in_sem.at[0])
     load_a.start()
+    load_pattern.start()
     for step in range(4):
         load_u(pair(step)).start()
 
@@ -88,6 +90,7 @@
     high, low = split(a_v[...].T)
     lhs[0:256] = high
     lhs[256:512] = low
+    load_pattern.wait()
 
     @pl.loop(0, 4)
     def _(step):
@@ -197,29 +200,41 @@
             (row, there_y * 4 + there_x),
         )
 
+    high, low = split(block * mask)
+    part = -jnp.dot(tb[...], jnp.concatenate([high, low], 0), preferred_element_type=F32)
+    part = part.reshape(16, 2, 16, 256)
+    for half in range(2):
+        ub[half] = part[:, half]
+    to_sibling = remote(ub.at[1 - q], ux, ux_send, ux_recv, sibling)
+    to_sibling.start()
+    to_sibling.wait_recv()
+
+    def to_col(t):
+        there = (row, 2 * t + q)
+        return (
+            remote(uq.at[t], ur.at[col], us_send.at[t], ur_recv, there),
+            remote(usc.at[t], ursc.at[col], uc_send.at[t], uc_recv, there),
+        )
+
+    sums_here = col % 2 == q
+
+    @pl.loop(0, 16)
+    def _(step):
+        t = (col // 2 + far_first(step, 16)) % 16
+        total = ub[q, t] + ux[t]
+        top = jnp.maximum(jnp.max(jnp.abs(total), axis=0, keepdims=True), TINY)
+        uq[t] = jnp.round(total * (TOP / top)).astype(jnp.int32).astype(I16)
+        usc[t] = top * (1.0 / TOP)
+
+        @pl.when(2 * t + q != col)
+        def _():
+            for copy in to_col(t):
+                copy.start()
+
     @pl.loop(0, 4)
     def _(kk):
         start(*im_args(kk))
 
-    high, low = split(block * mask)
-    part = -jnp.dot(tb[...], jnp.concatenate([high, low], 0), preferred_element_type=F32)
-    for half in range(2):
-        ub[half] = part[:, half * 128:(half + 1) * 128].reshape(32, 16, 128)
-    to_sibling = remote(ub.at[1 - q], ux, ux_send, ux_recv, sibling)
-    to_sibling.start()
-    to_sibling.wait_recv()
-    uo[...] = ub[q] + ux[...]
-
-    def to_col(step):
-        there = (col + far_first(step, 32)) % 32
-        return remote(uo.at[there], ur.at[col], us_send, ur_recv, (row, there))
-
-    @pl.loop(0, 31)
-    def _(step):
-        to_col(step).start()
-
-    ur[col] = uo[col]
-
     def ip_args(there):
         return (
             there == row,
@@ -229,6 +244,29 @@
 
     forwards_ip = jnp.logical_and((y % 4) // 2 == z % 2, y % 2 == q)
 
+    def to_row(step):
+        there = ((z + far_first(step, 8)) % 8 * 2 + q, col)
+        return remote(uf, up_all.at[z], uf_send.at[step], uf_recv, there)
+
+    finish = remote(fin, up_out, fin_send, fin_recv, sibling)
+
+    @pl.when(sums_here)
+    def _():
+        ur[col] = uq[col // 2]
+        ursc[col] = usc[col // 2]
+        arrival(ur.at[pl.ds(0, 31)], ur_recv).wait()
+        arrival(ursc.at[pl.ds(0, 31)], uc_recv).wait()
+        uf[...] = jnp.zeros_like(uf)
+
+        @pl.loop(0, 32)
+        def _(k):
+            uf[...] += ur[k].astype(jnp.int32).astype(F32) * ursc[k]
+
+        @pl.loop(0, 7)
+        def _(step):
+            to_row(step).start()
+        up_all[z] = uf[...]
+
     @pl.when(forwards_ip)
     def _():
         arrival(im, im_recv).wait()
@@ -237,20 +275,13 @@
         def _(step):
             start(*ip_args((row + 8 + step) % 16))
 
-    arrived = ur.at[pl.ds(0, 31)]
-    arrival(arrived, ur_recv).wait()
-    uf[...] = jnp.sum(ur[...], axis=0)
-
-    up_dst = up_all.at[row]
-
-    def to_row(step):
-        return remote(uf, up_dst, uf_send.at[step], uf_recv, ((row + far_first(step, 16)) % 16, col))
-
-    @pl.loop(0, 15)
-    def _(step):
-        to_row(step).start()
-
-    pltpu.make_async_copy(uf, up_dst, uf_recv).start()
+    @pl.when(sums_here)
+    def _():
+        arrival(up_all.at[pl.ds(0, 7)], uf_recv).wait()
+        for k in range(4):
+            fin[k // 2, :, (k % 2) * 256:(k % 2 + 1) * 256] = up_all[2 * k] + up_all[2 * k + 1]
+        finish.start()
+        pltpu.make_async_copy(fin, up_out, fin_recv).start()
 
     @pl.when(sends_pm)
     def _():
@@ -275,7 +306,13 @@
         sent(*im_args(kk))
 
     to_sibling.wait_send()
-    arrival(arrived, us_send).wait()
+
+    @pl.loop(0, 16)
+    def _(t):
+        @pl.when(2 * t + q != col)
+        def _():
+            for copy in to_col(t):
+                copy.wait_send()
 
     @pl.when(forwards_ip)
     def _():
@@ -283,15 +320,16 @@
         def _(there):
             sent(*ip_args(there))
 
-    @pl.loop(0, 15)
-    def _(step):
-        to_row(step).wait_send()
-
-    arrival(up_all, uf_recv).wait()
-    for k in range(8):
-        first = 4 * (k // 2) + k % 2
-        up_out[k // 4, :, (k % 4) * 128:(k % 4 + 1) * 128] = up_all[first] + up_all[first + 2]
+    @pl.when(sums_here)
+    def _():
+        @pl.loop(0, 7)
+        def _(step):
+            to_row(step).wait_send()
+
+        finish.wait_send()
+
     arrival(ip_out, ip_recv).wait()
+    arrival(up_out, fin_recv).wait()
 
 
 def shards(inverse_block, panels, pattern):
@@ -303,12 +341,13 @@
             jax.ShapeDtypeStruct((2, 16, 512), F32),
         ),
         in_specs=[
-            pl.BlockSpec(memory_space=pltpu.SMEM),
+            pl.BlockSpec(memory_space=pl.ANY),
             pl.BlockSpec(memory_space=pl.ANY),
             pl.BlockSpec(memory_space=pl.ANY),
         ],
-        out_specs=(pl.BlockSpec(memory_space=pl.ANY), pl.BlockSpec(memory_space=pltpu.VMEM)),
+        out_specs=(pl.BlockSpec(memory_space=pl.ANY), pl.BlockSpec(memory_space=pl.ANY)),
         scratch_shapes=[
+            pltpu.SMEM((2, 64), jnp.int32),
             pltpu.VMEM((512, 256), F32),
             pltpu.VMEM((4, 512, 256), BF16),
             pltpu.VMEM((512, 512), BF16),
@@ -323,18 +362,21 @@
             pltpu.VMEM((8, 1, 256), F32),
             pltpu.VMEM((64, 256), F32),
             pltpu.VMEM((16, 16, 256), F32),
-            pltpu.VMEM((2, 32, 16, 128), F32),
-            pltpu.VMEM((32, 16, 128), F32),
-            pltpu.VMEM((32, 16, 128), F32),
-            pltpu.VMEM((32, 16, 128), F32),
-            pltpu.VMEM((16, 128), F32),
+            pltpu.VMEM((2, 16, 16, 256), F32),
+            pltpu.VMEM((16, 16, 256), F32),
+            pltpu.VMEM((16, 16, 256), I16),
+            pltpu.VMEM((16, 1, 256), F32),
+            pltpu.VMEM((32, 16, 256), I16),
+            pltpu.VMEM((32, 1, 256), F32),
+            pltpu.VMEM((16, 256), F32),
             pltpu.VMEM((64, 256), F32),
-            pltpu.VMEM((16, 16, 128), F32),
-            dma((5,)), dma((2,)), dma((2,)), dma((2,)), dma, dma((4,)), dma((4,)), dma((8,)), dma((8,)), dma((8,)),
-            dma((8,)), dma((4,)), dma, dma((16,)), dma, dma, dma, dma, dma, dma((16,)), dma,
+            pltpu.VMEM((8, 16, 256), F32),
+            pltpu.VMEM((2, 16, 512), F32),
+            dma((6,)), dma((2,)), dma((2,)), dma((2,)), dma, dma((4,)), dma((4,)), dma((8,)), dma((8,)), dma((8,)),
+            dma((8,)), dma((4,)), dma, dma((16,)), dma, dma, dma, dma((16,)), dma, dma((16,)), dma, dma((7,)), dma, dma, dma,
         ],
         compiler_params=pltpu.CompilerParams(
-            collective_id=0, has_side_effects=True, vmem_limit_bytes=60 * 1024 * 1024
+            collective_id=0, has_side_effects=True, vmem_limit_bytes=56250000
         ),
         cost_estimate=pl.CostEstimate(flops=2 ** 29, bytes_accessed=2 ** 21, transcendentals=0),
     )(pattern, inverse_block, panels)

time: 52.3 us -> 51.2 us (0.979)
  Pallas kernels: 49.3 us -> 48.5 us
    pallas_call x1, Pallas kernels: 49.3 us -> 48.5 us  [shards(): pl.pallas_call(kernel, out_shape=(jax.ShapeDtypeStruct((2, 16, 512), F32)...]
where the time goes in v4:
time: 51.2 us; the launch traced here: 51 us
  Pallas kernels  48.5 us (95%)
  local copies, waits for them, and re-layouts  1.93 us (4%)
  between operations  0.65 us (1%)
    pallas_call x1, Pallas kernels, shards(): pl.pallas_call(kernel, out_shape=(jax.ShapeDtypeStruct((2, 16, 512), F32)...  48.5 us
    unnamed x4, local copies, waits for them, and re-layouts  1.93 us

profile of v4, /device:TPU:1, one launch (start us, length us, event | category | flops | bytes accessed | tf_op | source)
XLA Modules:
  0.0 51.0 jit_solution(15834021066239671183)
XLA Ops:
  0.6 0.0 copy-start
  0.6 0.7 %copy-done = s32[2,64]{1,0:T(2,128)S(1)} copy-done((s32[2,64]{1,0:T(2,128)S(1)}, s32[2,64]{1,0:T(2,128)}, u32[]{:S(2)}) %copy-start) | copy-done | bytes 536
  1.3 48.5 %shard_map.50 = (f32[2,16,512]{2,1,0:T(8,128)S(1)}, f32[2,16,512]{2,1,0:T(8,128)S(1)}) custom-call(s32[2,64]{1,0:T(2,128)S(1)} %copy-done, f32[512,256]{1,0:T(8,128)} %a_hbm.1, bf16[2,512,512]{2,1,0:T(8,128)(2,1)} %panels_hbm.1), custom_call_target="tpu_custom_call" | custom-call | flops 536870912 | bytes 2097152 | tf_op jit(solution)/shard_map/pallas_call | solution.py:337
  49.8 0.6 %copy.7 = f32[2,16,512]{2,1,0:T(8,128)} copy(f32[2,16,512]{2,1,0:T(8,128)S(1)} %get-tuple-element.4) | data formatting | bytes 131072
  50.4 0.6 %copy.8 = f32[2,16,512]{2,1,0:T(8,128)} copy(f32[2,16,512]{2,1,0:T(8,128)S(1)} %get-tuple-element.5) | data formatting | bytes 131072
Async XLA Ops:
  0.6 0.7 %copy-start = (s32[2,64]{1,0:T(2,128)S(1)}, s32[2,64]{1,0:T(2,128)}, u32[]{:S(2)}) copy-start(s32[2,64]{1,0:T(2,128)} %pattern_hbm.1) | copy-start | bytes 1540

commit v5 on v4

--- a/solution.py
+++ b/solution.py
@@ -25,7 +25,7 @@
     pattern_hbm, a_hbm, panels_hbm, ip_out, up_out,
     pattern, a_v, u_v, lhs, pm, pf, tb, pb, xb, zs, zsc, zr, zrsc, own, im, ub, ux, uq, usc, ur, ursc, uf, ipo, up_all, fin,
     in_sem, pm_send, pm_recv, pf_send, pf_recv, xs_send, xs_recv, zs_send, zr_recv, zc_send, zc_recv,
-    im_send, im_recv, ip_send, ip_recv, ux_send, ux_recv, us_send, ur_recv, uc_send, uc_recv, uf_send, uf_recv, fin_send, fin_recv,
+    im_send, im_recv, ip_send, ip_recv, ux_send, ux_recv, us_send, ur_recv, uc_send, uc_recv, uf_send, uf_recv, fin_send, fin_recv, ready,
 ):
     row = lax.axis_index("row")
     col = lax.axis_index("col")
@@ -76,15 +76,54 @@
 
     barrier = pltpu.get_barrier_semaphore()
 
+    @pl.loop(0, 7)
+    def _(step):
+        there = ((z + far_first(step, 8)) % 8 * 2, col)
+        pl.semaphore_signal(barrier, inc=1, device_id=there, device_id_type=MESH)
+
+    @pl.when(q == 1)
+    def _():
+        pl.semaphore_signal(barrier, inc=1, device_id=sibling, device_id_type=MESH)
+
     @pl.loop(0, 31)
     def _(step):
-        there = (row, (col + far_first(step, 32)) % 32)
+        there = (z * 2 + 1, (col + far_first(step, 32)) % 32)
         pl.semaphore_signal(barrier, inc=1, device_id=there, device_id_type=MESH)
 
-    @pl.loop(0, 15)
-    def _(step):
-        there = ((row + far_first(step, 16)) % 16, col)
-        pl.semaphore_signal(barrier, inc=1, device_id=there, device_id_type=MESH)
+    def hear(core, count):
+        @pl.when(q == core)
+        def _():
+            pl.semaphore_wait(barrier, count)
+            pl.semaphore_signal(ready, inc=1, device_id=sibling, device_id_type=MESH)
+
+        @pl.when(q != core)
+        def _():
+            pl.semaphore_wait(ready, 1)
+
+    hear(0, 15)
+
+    pm_z = (2 * z + 12 - y) % 8
+    pm_slot = ((y + 9 - z) % 8) // 4
+    sends_pm = q == x // 2
+    hands_on = (y + z) % 2 == 0
+
+    def pm_args(core):
+        first = (x % 2) * 256 + (pm_z % 2) * 128 + core * 64
+        return (
+            jnp.logical_and(pm_z == z, q == core),
+            panels_hbm.at[pm_z // 4, pl.ds(pl.multiple_of(first, 64), 64), :], pm.at[pm_slot],
+            pm_send.at[core], pm_recv.at[pm_slot], (pm_z * 2 + core, col),
+        )
+
+    def pf_args(turn):
+        via = ((y + z) // 2 + 2 + 4 * turn) % 8
+        slot = ((y + 9 - via) % 8) // 4
+        return slot, (via == y, pm.at[slot], pf, pf_send.at[slot], pf_recv, (row, via * 4 + x))
+
+    @pl.when(sends_pm)
+    def _():
+        for core in range(2):
+            start(*pm_args(core))
 
     load_a.wait()
     high, low = split(a_v[...].T)
@@ -107,31 +146,6 @@
                 first = which * 128 + half * 64
                 pb[half, 2 * p + which] = product[first:first + 64]
 
-    pl.semaphore_wait(barrier, 46)
-
-    pm_z = (2 * z + 12 - y) % 8
-    pm_slot = ((y + 9 - z) % 8) // 4
-    sends_pm = q == x // 2
-    hands_on = (y + z) % 2 == 0
-
-    def pm_args(core):
-        first = (x % 2) * 256 + (pm_z % 2) * 128 + core * 64
-        return (
-            jnp.logical_and(pm_z == z, q == core),
-            panels_hbm.at[pm_z // 4, pl.ds(pl.multiple_of(first, 64), 64), :], pm.at[pm_slot],
-            pm_send.at[core], pm_recv.at[pm_slot], (pm_z * 2 + core, col),
-        )
-
-    def pf_args(turn):
-        via = ((y + z) // 2 + 2 + 4 * turn) % 8
-        slot = ((y + 9 - via) % 8) // 4
-        return slot, (via == y, pm.at[slot], pf, pf_send.at[slot], pf_recv, (row, via * 4 + x))
-
-    @pl.when(sends_pm)
-    def _():
-        for core in range(2):
-            start(*pm_args(core))
-
     def exchange(p):
         return remote(
             pb.at[1 - q, pl.ds(2 * p, 2)], xb.at[pl.ds(2 * p, 2)], xs_send.at[p], xs_recv.at[p], sibling
@@ -147,6 +161,15 @@
             remote(zsc.at[d], zrsc.at[z], zc_send.at[d], zc_recv.at[z], there),
         )
 
+    hear(1, 62)
+
+    @pl.when(hands_on)
+    def _():
+        for turn in range(2):
+            slot, args = pf_args(turn)
+            arrival(pm.at[slot], pm_recv.at[slot]).wait()
+            start(*args)
+
     @pl.loop(0, 8)
     def _(step):
         p, which = pair(step // 2), step % 2
@@ -169,13 +192,6 @@
             zsc[d] = top * (1.0 / TOP)
             for copy in to_z(d):
                 copy.start()
-
-    @pl.when(hands_on)
-    def _():
-        for turn in range(2):
-            slot, args = pf_args(turn)
-            arrival(pm.at[slot], pm_recv.at[slot]).wait()
-            start(*args)
 
     arrival(pf, pf_recv).wait()
     flipped = pf[...].T
@@ -374,6 +390,7 @@
             pltpu.VMEM((2, 16, 512), F32),
             dma((6,)), dma((2,)), dma((2,)), dma((2,)), dma, dma((4,)), dma((4,)), dma((8,)), dma((8,)), dma((8,)),
             dma((8,)), dma((4,)), dma, dma((16,)), dma, dma, dma, dma((16,)), dma, dma((16,)), dma, dma((7,)), dma, dma, dma,
+            pltpu.SemaphoreType.REGULAR,
         ],
         compiler_params=pltpu.CompilerParams(
             collective_id=0, has_side_effects=True, vmem_limit_bytes=56250000

time: 51.2 us -> 48 us (0.938)
  Pallas kernels: 48.5 us -> 45.3 us
    pallas_call x1, Pallas kernels: 48.5 us -> 45.3 us  [shards(): pl.pallas_call(kernel, out_shape=(jax.ShapeDtypeStruct((2, 16, 512), F32)...]
where the time goes in v5:
time: 48 us; the launch traced here: 47.9 us
  Pallas kernels  45.3 us (94%)
  local copies, waits for them, and re-layouts  1.93 us (4%)
  between operations  0.65 us (1%)
    pallas_call x1, Pallas kernels, shards(): pl.pallas_call(kernel, out_shape=(jax.ShapeDtypeStruct((2, 16, 512), F32)...  45.3 us
    unnamed x4, local copies, waits for them, and re-layouts  1.93 us

profile of v5, /device:TPU:1, one launch (start us, length us, event | category | flops | bytes accessed | tf_op | source)
XLA Modules:
  0.0 47.9 jit_solution(6026915849708276898)
XLA Ops:
  0.6 0.0 copy-start
  0.6 0.7 %copy-done = s32[2,64]{1,0:T(2,128)S(1)} copy-done((s32[2,64]{1,0:T(2,128)S(1)}, s32[2,64]{1,0:T(2,128)}, u32[]{:S(2)}) %copy-start) | copy-done | bytes 536
  1.3 45.3 %shard_map.50 = (f32[2,16,512]{2,1,0:T(8,128)S(1)}, f32[2,16,512]{2,1,0:T(8,128)S(1)}) custom-call(s32[2,64]{1,0:T(2,128)S(1)} %copy-done, f32[512,256]{1,0:T(8,128)} %a_hbm.1, bf16[2,512,512]{2,1,0:T(8,128)(2,1)} %panels_hbm.1), custom_call_target="tpu_custom_call" | custom-call | flops 536870912 | bytes 2097152 | tf_op jit(solution)/shard_map/pallas_call | solution.py:353
  46.6 0.6 %copy.7 = f32[2,16,512]{2,1,0:T(8,128)} copy(f32[2,16,512]{2,1,0:T(8,128)S(1)} %get-tuple-element.4) | data formatting | bytes 131072
  47.3 0.6 %copy.8 = f32[2,16,512]{2,1,0:T(8,128)} copy(f32[2,16,512]{2,1,0:T(8,128)S(1)} %get-tuple-element.5) | data formatting | bytes 131072
Async XLA Ops:
  0.6 0.7 %copy-start = (s32[2,64]{1,0:T(2,128)S(1)}, s32[2,64]{1,0:T(2,128)}, u32[]{:S(2)}) copy-start(s32[2,64]{1,0:T(2,128)} %pattern_hbm.1) | copy-start | bytes 1540

commit v6 on v5

--- a/solution.py
+++ b/solution.py
@@ -23,7 +23,7 @@
 
 def kernel(
     pattern_hbm, a_hbm, panels_hbm, ip_out, up_out,
-    pattern, a_v, u_v, lhs, pm, pf, tb, pb, xb, zs, zsc, zr, zrsc, own, im, ub, ux, uq, usc, ur, ursc, uf, ipo, up_all, fin,
+    pattern, a_v, u_v, lhs, pm, pf, tb, pb, xb, zs, zsc, zr, zrsc, own, im, ub_rhs, ub, ux, uq, usc, ur, ursc, uf, ipo, up_all, fin,
     in_sem, pm_send, pm_recv, pf_send, pf_recv, xs_send, xs_recv, zs_send, zr_recv, zc_send, zc_recv,
     im_send, im_recv, ip_send, ip_recv, ux_send, ux_recv, us_send, ur_recv, uc_send, uc_recv, uf_send, uf_recv, fin_send, fin_recv, ready,
 ):
@@ -209,21 +209,23 @@
     ipo[...] = block
 
     def im_args(kk):
-        there_x, there_y = kk, (x % 2) * 4 + (z % 2) * 2 + q
+        there_x, there_y, there_q = kk, (x % 2) * 4 + (z % 2) * 2 + q, y % 2
         return (
-            jnp.logical_and(there_x == x, there_y == y),
-            ipo.at[pl.ds(pl.multiple_of(kk * 16, 16), 16)], im.at[y * 2 + x // 2], im_send.at[kk], im_recv,
-            (row, there_y * 4 + there_x),
+            jnp.logical_and(there_q == q, jnp.logical_and(there_x == x, there_y == y)),
+            ipo.at[pl.ds(pl.multiple_of(kk * 16, 16), 16)], im.at[y // 2 * 2 + x // 2], im_send.at[kk], im_recv,
+            (z * 2 + there_q, there_y * 4 + there_x),
         )
 
     high, low = split(block * mask)
-    part = -jnp.dot(tb[...], jnp.concatenate([high, low], 0), preferred_element_type=F32)
-    part = part.reshape(16, 2, 16, 256)
-    for half in range(2):
-        ub[half] = part[:, half]
-    to_sibling = remote(ub.at[1 - q], ux, ux_send, ux_recv, sibling)
-    to_sibling.start()
-    to_sibling.wait_recv()
+    ub_rhs[0:64] = -high
+    ub_rhs[64:128] = -low
+
+    def quarter(step):
+        return (y // 2 + jnp.where(step == 0, 2, jnp.where(step == 3, 0, 2 * step - 1))) % 4
+
+    def to_sibling(g):
+        some = pl.ds(4 * g, 4)
+        return remote(ub.at[1 - q, some], ux.at[some], ux_send.at[g], ux_recv.at[g], sibling)
 
     def to_col(t):
         there = (row, 2 * t + q)
@@ -232,33 +234,49 @@
             remote(usc.at[t], ursc.at[col], uc_send.at[t], uc_recv, there),
         )
 
+    @pl.loop(0, 4, unroll=True)
+    def _(step):
+        g = quarter(step)
+        part = jnp.dot(
+            tb[pl.ds(pl.multiple_of(g * 128, 128), 128)], ub_rhs[...], preferred_element_type=F32
+        ).reshape(4, 2, 16, 256)
+        for half in range(2):
+            ub[half, pl.ds(4 * g, 4)] = part[:, half]
+        to_sibling(g).start()
+
     sums_here = col % 2 == q
 
-    @pl.loop(0, 16)
-    def _(step):
-        t = (col // 2 + far_first(step, 16)) % 16
-        total = ub[q, t] + ux[t]
-        top = jnp.maximum(jnp.max(jnp.abs(total), axis=0, keepdims=True), TINY)
-        uq[t] = jnp.round(total * (TOP / top)).astype(jnp.int32).astype(I16)
-        usc[t] = top * (1.0 / TOP)
-
-        @pl.when(2 * t + q != col)
-        def _():
-            for copy in to_col(t):
-                copy.start()
+    @pl.loop(0, 4)
+    def _(step):
+        g = quarter(step)
+        to_sibling(g).wait_recv()
+        for one in range(4):
+            t = 4 * g + one
+            total = ub[q, t] + ux[t]
+            top = jnp.maximum(jnp.max(jnp.abs(total), axis=0, keepdims=True), TINY)
+            uq[t] = jnp.round(total * (TOP / top)).astype(jnp.int32).astype(I16)
+            usc[t] = top * (1.0 / TOP)
+        for one in range(4):
+            t = 4 * g + one
+
+            @pl.when(2 * t + q != col)
+            def _():
+                for copy in to_col(t):
+                    copy.start()
 
     @pl.loop(0, 4)
     def _(kk):
         start(*im_args(kk))
 
-    def ip_args(there):
+    def ip_args(k):
+        there = (k // 2 * 2 + q) * 2 + k % 2
         return (
             there == row,
-            im.at[there], ip_out.at[z // 4, :, pl.ds(pl.multiple_of((z // 2 % 2) * 256, 256), 256)],
-            ip_send.at[there], ip_recv, (there, col),
-        )
-
-    forwards_ip = jnp.logical_and((y % 4) // 2 == z % 2, y % 2 == q)
+            im.at[k], ip_out.at[z // 4, :, pl.ds(pl.multiple_of((z // 2 % 2) * 256, 256), 256)],
+            ip_send.at[k], ip_recv, (there, col),
+        )
+
+    forwards_ip = (y % 4) // 2 == z % 2
 
     def to_row(step):
         there = ((z + far_first(step, 8)) % 8 * 2 + q, col)
@@ -287,9 +305,9 @@
     def _():
         arrival(im, im_recv).wait()
 
-        @pl.loop(0, 16)
+        @pl.loop(0, 8)
         def _(step):
-            start(*ip_args((row + 8 + step) % 16))
+            start(*ip_args((z // 2 * 2 + 4 + step) % 8))
 
     @pl.when(sums_here)
     def _():
@@ -321,7 +339,8 @@
     def _(kk):
         sent(*im_args(kk))
 
-    to_sibling.wait_send()
+    for g in range(4):
+        to_sibling(g).wait_send()
 
     @pl.loop(0, 16)
     def _(t):
@@ -332,9 +351,9 @@
 
     @pl.when(forwards_ip)
     def _():
-        @pl.loop(0, 16)
-        def _(there):
-            sent(*ip_args(there))
+        @pl.loop(0, 8)
+        def _(k):
+            sent(*ip_args(k))
 
     @pl.when(sums_here)
     def _():
@@ -356,11 +375,7 @@
             jax.ShapeDtypeStruct((2, 16, 512), F32),
             jax.ShapeDtypeStruct((2, 16, 512), F32),
         ),
-        in_specs=[
-            pl.BlockSpec(memory_space=pl.ANY),
-            pl.BlockSpec(memory_space=pl.ANY),
-            pl.BlockSpec(memory_space=pl.ANY),
-        ],
+        in_specs=[pl.BlockSpec(memory_space=pltpu.HBM)] * 3,
         out_specs=(pl.BlockSpec(memory_space=pl.ANY), pl.BlockSpec(memory_space=pl.ANY)),
         scratch_shapes=[
             pltpu.SMEM((2, 64), jnp.int32),
@@ -377,7 +392,8 @@
             pltpu.VMEM((8, 64, 256), I16),
             pltpu.VMEM((8, 1, 256), F32),
             pltpu.VMEM((64, 256), F32),
-            pltpu.VMEM((16, 16, 256), F32),
+            pltpu.VMEM((8, 16, 256), F32),
+            pltpu.VMEM((128, 256), BF16),
             pltpu.VMEM((2, 16, 16, 256), F32),
             pltpu.VMEM((16, 16, 256), F32),
             pltpu.VMEM((16, 16, 256), I16),
@@ -389,7 +405,7 @@
             pltpu.VMEM((8, 16, 256), F32),
             pltpu.VMEM((2, 16, 512), F32),
             dma((6,)), dma((2,)), dma((2,)), dma((2,)), dma, dma((4,)), dma((4,)), dma((8,)), dma((8,)), dma((8,)),
-            dma((8,)), dma((4,)), dma, dma((16,)), dma, dma, dma, dma((16,)), dma, dma((16,)), dma, dma((7,)), dma, dma, dma,
+            dma((8,)), dma((4,)), dma, dma((8,)), dma, dma((4,)), dma((4,)), dma((16,)), dma, dma((16,)), dma, dma((7,)), dma, dma, dma,
             pltpu.SemaphoreType.REGULAR,
         ],
         compiler_params=pltpu.CompilerParams(

time: 48 us -> 46.7 us (0.973); the launches traced: 47.9 us -> 45.9 us
  Pallas kernels: 45.3 us -> 43.4 us
    pallas_call x1, Pallas kernels: 45.3 us -> 43.4 us  [shards(): pl.pallas_call(kernel, out_shape=(jax.ShapeDtypeStruct((2, 16, 512), F32)...]
where the time goes in v6:
time: 46.7 us; the launch traced here: 45.9 us
  Pallas kernels  43.4 us (93%)
  local copies, waits for them, and re-layouts  1.93 us (4%)
  between operations  0.65 us (1%)
    pallas_call x1, Pallas kernels, shards(): pl.pallas_call(kernel, out_shape=(jax.ShapeDtypeStruct((2, 16, 512), F32)...  43.4 us
    unnamed x4, local copies, waits for them, and re-layouts  1.93 us

profile of v6, /device:TPU:1, one launch (start us, length us, event | category | flops | bytes accessed | tf_op | source)
XLA Modules:
  0.0 45.9 jit_solution(808021151470427055)
XLA Ops:
  0.6 0.0 copy-start
  0.6 0.7 %copy-done = s32[2,64]{1,0:T(2,128)S(1)} copy-done((s32[2,64]{1,0:T(2,128)S(1)}, s32[2,64]{1,0:T(2,128)}, u32[]{:S(2)}) %copy-start) | copy-done | bytes 536
  1.3 43.4 %shard_map.50 = (f32[2,16,512]{2,1,0:T(8,128)S(1)}, f32[2,16,512]{2,1,0:T(8,128)S(1)}) custom-call(s32[2,64]{1,0:T(2,128)S(1)} %copy-done, f32[512,256]{1,0:T(8,128)} %a_hbm.1, bf16[2,512,512]{2,1,0:T(8,128)(2,1)} %panels_hbm.1), custom_call_target="tpu_custom_call" | custom-call | flops 536870912 | bytes 2097152 | tf_op jit(solution)/shard_map/pallas_call | solution.py:372
  44.7 0.6 %copy.7 = f32[2,16,512]{2,1,0:T(8,128)} copy(f32[2,16,512]{2,1,0:T(8,128)S(1)} %get-tuple-element.4) | data formatting | bytes 131072
  45.3 0.6 %copy.8 = f32[2,16,512]{2,1,0:T(8,128)} copy(f32[2,16,512]{2,1,0:T(8,128)S(1)} %get-tuple-element.5) | data formatting | bytes 131072
Async XLA Ops:
  0.6 0.7 %copy-start = (s32[2,64]{1,0:T(2,128)S(1)}, s32[2,64]{1,0:T(2,128)}, u32[]{:S(2)}) copy-start(s32[2,64]{1,0:T(2,128)} %pattern_hbm.1) | copy-start | bytes 1540

commit v7 on v6

--- a/solution.py
+++ b/solution.py
@@ -22,11 +22,12 @@
 
 
 def kernel(
-    pattern_hbm, a_hbm, panels_hbm, ip_out, up_out,
+    pattern_hbm, a_hbm, panels_hbm, both_out,
     pattern, a_v, u_v, lhs, pm, pf, tb, pb, xb, zs, zsc, zr, zrsc, own, im, ub_rhs, ub, ux, uq, usc, ur, ursc, uf, ipo, up_all, fin,
     in_sem, pm_send, pm_recv, pf_send, pf_recv, xs_send, xs_recv, zs_send, zr_recv, zc_send, zc_recv,
     im_send, im_recv, ip_send, ip_recv, ux_send, ux_recv, us_send, ur_recv, uc_send, uc_recv, uf_send, uf_recv, fin_send, fin_recv, ready,
 ):
+    ip_out, up_out = both_out.at[0], both_out.at[1]
     row = lax.axis_index("row")
     col = lax.axis_index("col")
     z, q = row // 2, row % 2
@@ -369,14 +370,11 @@
 
 def shards(inverse_block, panels, pattern):
     dma = pltpu.SemaphoreType.DMA
-    return pl.pallas_call(
+    both = pl.pallas_call(
         kernel,
-        out_shape=(
-            jax.ShapeDtypeStruct((2, 16, 512), F32),
-            jax.ShapeDtypeStruct((2, 16, 512), F32),
-        ),
+        out_shape=jax.ShapeDtypeStruct((2, 2, 16, 512), F32),
         in_specs=[pl.BlockSpec(memory_space=pltpu.HBM)] * 3,
-        out_specs=(pl.BlockSpec(memory_space=pl.ANY), pl.BlockSpec(memory_space=pl.ANY)),
+        out_specs=pl.BlockSpec(memory_space=pl.ANY),
         scratch_shapes=[
             pltpu.SMEM((2, 64), jnp.int32),
             pltpu.VMEM((512, 256), F32),
@@ -413,6 +411,7 @@
         ),
         cost_estimate=pl.CostEstimate(flops=2 ** 29, bytes_accessed=2 ** 21, transcendentals=0),
     )(pattern, inverse_block, panels)
+    return both[0], both[1]
 
 
 def solution(mesh):

time: 46.7 us -> 46.1 us (0.987)
  local copies, waits for them, and re-layouts: 1.93 us -> 1.33 us
    unnamed x4 -> x2, local copies, waits for them, and re-layouts: 1.93 us -> 0.67 us
    squeeze x0 -> x1, local copies, waits for them, and re-layouts: none -> 0.66 us  [shards(): return (both[0], both[1])]
where the time goes in v7:
time: 46.1 us; the launch traced here: 45.3 us
  Pallas kernels  43.4 us (94%)
  local copies, waits for them, and re-layouts  1.33 us (3%)
  between operations  0.65 us (1%)
    pallas_call x1, Pallas kernels, shards(): pl.pallas_call(kernel, out_shape=jax.ShapeDtypeStruct((2, 2, 16, 512), F3...  43.4 us

profile of v7, /device:TPU:1, one launch (start us, length us, event | category | flops | bytes accessed | tf_op | source)
XLA Modules:
  0.0 45.3 jit_solution(4957497260832713734)
XLA Ops:
  0.6 0.0 copy-start
  0.6 0.7 %copy-done = s32[2,64]{1,0:T(2,128)S(1)} copy-done((s32[2,64]{1,0:T(2,128)S(1)}, s32[2,64]{1,0:T(2,128)}, u32[]{:S(2)}) %copy-start) | copy-done | bytes 536
  1.3 43.4 %shard_map.50 = f32[2,2,16,512]{3,2,1,0:T(8,128)S(1)} custom-call(s32[2,64]{1,0:T(2,128)S(1)} %copy-done, f32[512,256]{1,0:T(8,128)} %a_hbm.1, bf16[2,512,512]{2,1,0:T(8,128)(2,1)} %panels_hbm.1), custom_call_target="tpu_custom_call" | custom-call | flops 536870912 | bytes 2097152 | tf_op jit(solution)/shard_map/pallas_call | solution.py:373
  44.7 0.7 %slice_bitcast_fusion = (f32[2,16,512]{2,1,0:T(8,128)}, f32[2,16,512]{2,1,0:T(8,128)}) fusion(f32[2,2,16,512]{3,2,1,0:T(8,128)S(1)} %shard_map.50), kind=kLoop, calls=%fused_computation | loop fusion | bytes 262144 | tf_op jit(solution)/shard_map/squeeze | solution.py:414
Async XLA Ops:
  0.6 0.7 %copy-start = (s32[2,64]{1,0:T(2,128)S(1)}, s32[2,64]{1,0:T(2,128)}, u32[]{:S(2)}) copy-start(s32[2,64]{1,0:T(2,128)} %pattern_hbm.1) | copy-start | bytes 1540

commit v8 on v7

--- a/solution.py
+++ b/solution.py
@@ -101,6 +101,12 @@
         def _():
             pl.semaphore_wait(ready, 1)
 
+    load_a.wait()
+    high, low = split(a_v[...].T)
+    lhs[0:256] = high
+    lhs[256:512] = low
+    load_pattern.wait()
+
     hear(0, 15)
 
     pm_z = (2 * z + 12 - y) % 8
@@ -125,12 +131,6 @@
     def _():
         for core in range(2):
             start(*pm_args(core))
-
-    load_a.wait()
-    high, low = split(a_v[...].T)
-    lhs[0:256] = high
-    lhs[256:512] = low
-    load_pattern.wait()
 
     @pl.loop(0, 4)
     def _(step):
@@ -291,11 +291,10 @@
         ursc[col] = usc[col // 2]
         arrival(ur.at[pl.ds(0, 31)], ur_recv).wait()
         arrival(ursc.at[pl.ds(0, 31)], uc_recv).wait()
-        uf[...] = jnp.zeros_like(uf)
-
-        @pl.loop(0, 32)
-        def _(k):
-            uf[...] += ur[k].astype(jnp.int32).astype(F32) * ursc[k]
+        def add(k, total):
+            return total + ur[k].astype(jnp.int32).astype(F32) * ursc[k]
+
+        uf[...] = lax.fori_loop(0, 32, add, jnp.zeros((16, 256), F32), unroll=8)
 
         @pl.loop(0, 7)
         def _(step):

time: 46.1 us -> 46.1 us (level); the launches traced: 45.3 us -> 45.9 us
  Pallas kernels: 43.4 us -> 43.9 us
    pallas_call x1, Pallas kernels: 43.4 us -> 43.9 us  [shards(): pl.pallas_call(kernel, out_shape=jax.ShapeDtypeStruct((2, 2, 16, 512), F3...]
where the time goes in v8:
time: 46.1 us; the launch traced here: 45.9 us
  Pallas kernels  43.9 us (95%)
  local copies, waits for them, and re-layouts  1.33 us (3%)
  between operations  0.65 us (1%)
    pallas_call x1, Pallas kernels, shards(): pl.pallas_call(kernel, out_shape=jax.ShapeDtypeStruct((2, 2, 16, 512), F3...  43.9 us

profile of v8, /device:TPU:1, one launch (start us, length us, event | category | flops | bytes accessed | tf_op | source)
XLA Modules:
  0.0 45.9 jit_solution(12713555701676283191)
XLA Ops:
  0.6 0.0 copy-start
  0.6 0.7 %copy-done = s32[2,64]{1,0:T(2,128)S(1)} copy-done((s32[2,64]{1,0:T(2,128)S(1)}, s32[2,64]{1,0:T(2,128)}, u32[]{:S(2)}) %copy-start) | copy-done | bytes 536
  1.3 43.9 %shard_map.50 = f32[2,2,16,512]{3,2,1,0:T(8,128)S(1)} custom-call(s32[2,64]{1,0:T(2,128)S(1)} %copy-done, f32[512,256]{1,0:T(8,128)} %a_hbm.1, bf16[2,512,512]{2,1,0:T(8,128)(2,1)} %panels_hbm.1), custom_call_target="tpu_custom_call" | custom-call | flops 536870912 | bytes 2097152 | tf_op jit(solution)/shard_map/pallas_call | solution.py:372
  45.3 0.7 %slice_bitcast_fusion = (f32[2,16,512]{2,1,0:T(8,128)}, f32[2,16,512]{2,1,0:T(8,128)}) fusion(f32[2,2,16,512]{3,2,1,0:T(8,128)S(1)} %shard_map.50), kind=kLoop, calls=%fused_computation | loop fusion | bytes 262144 | tf_op jit(solution)/shard_map/squeeze | solution.py:413
Async XLA Ops:
  0.6 0.7 %copy-start = (s32[2,64]{1,0:T(2,128)S(1)}, s32[2,64]{1,0:T(2,128)}, u32[]{:S(2)}) copy-start(s32[2,64]{1,0:T(2,128)} %pattern_hbm.1) | copy-start | bytes 1540
